TPU v7x, 256 devices: a whole 4x4x8 slice. The times are simulated.
256 devices in a mesh: pipe: 4 (over y), dp: 32 (over z, x), tensor: 2 (over core).
Axes of the slice: x: 4, y: 4, z: 8, core: 2. Of those that a mesh axis runs over, the one named last changes fastest.
Arguments:
- llm_grad: bfloat16 [4, 1024, 1664], P(None, 'dp'), may hold values from -6 to 6
- slot_row: int32 [4, 32, 32], P(None, 'dp'), may hold values from 0 to 31, each once within a row
- counts: int32 [32, 4], P('dp'), may hold values from 8 to 32, as said below
- saved_in: bfloat16 [4, 4, 1024, 1664], P('pipe', None, 'dp'), may hold values from -6 to 6
- saved_pre: bfloat16 [4, 4, 1024, 6400], P('pipe', None, 'dp', 'tensor'), may hold values from -6 to 6
- weights: bfloat16 [4, 1664, 6400], P('pipe', 'dp', 'tensor'), may hold values from -0.15625 to 0.15625
- channel_scale: float32 [4, 1664], P('pipe'), may hold values from 0.25 to 2
Outputs:
- weight_grad: bfloat16 [4, 1664, 6400], P('pipe', 'dp', 'tensor')
- section_grad: bfloat16 [4, 4, 1024, 1664], P('pipe', None, 'dp')
Inputs may be any that keep to these rules, and one draw needn't show every extreme that they name: For each micro-batch and rank, slot_row lists every row of the rank once. `counts`: both ends of the range occur in every draw.
All inputs are finite; a program needn't handle non-finite values.
Results may differ from a plain program's by a relative error of at most 0.023.
Values may be sent and summed in bfloat16 or wider, within the bound.
A program may use at most 128 MiB of HBM per device.

v0:
```python
import jax
import jax.numpy as jnp
from jax import lax
from jax.sharding import PartitionSpec as P

norm_eps = 1e-06
root_half = 0.7071067811865476
inv_root_two_pi = 0.3989422804014327


def shortened(value):

    def short(part):
        return part.astype(jnp.bfloat16) if part.dtype == jnp.float32 else part

    return jax.tree.map(short, value)


def shifted(block, axis, distance):
    devices = range(lax.axis_size(axis))
    route = [(i - distance, i) for i in devices if i - distance in devices]
    return lax.ppermute(block, axis, route)


def gelu_parts(pre_act):
    normal_cdf = 0.5 * (1.0 + jax.scipy.special.erf(pre_act * root_half))
    density = jnp.exp(-0.5 * pre_act * pre_act) * inv_root_two_pi
    return (pre_act * normal_cdf, normal_cdf + pre_act * density)


def local_top(llm_grad, slot_row, counts):
    row_count = llm_grad.shape[1]
    slot_ids = jnp.arange(row_count, dtype=jnp.int32)
    kept_mask = slot_ids[None, :] < counts[:, None]
    source = jnp.where(kept_mask[..., None], llm_grad, jnp.zeros_like(llm_grad))
    onehot = (slot_row[:, :, None] == slot_ids[None, None, :]).astype(jnp.bfloat16)
    placed = jnp.einsum("mjr,mjd->mrd", onehot, source, preferred_element_type=jnp.float32)
    return placed.astype(jnp.bfloat16)


def norm_back(incoming, dnorm, unit_rows, inv_std, channel_gain):
    scaled_back = dnorm * channel_gain
    back = inv_std * (
        scaled_back
        - jnp.mean(scaled_back, axis=-1, keepdims=True)
        - unit_rows * jnp.mean(scaled_back * unit_rows, axis=-1, keepdims=True)
    )
    return (incoming.astype(jnp.float32) + back).astype(jnp.bfloat16)


def add_term(grad_total, left_side, right_side):
    return grad_total + lax.dot_general(
        left_side, right_side, (((0,), (0,)), ((), ())), preferred_element_type=jnp.float32
    )


def keep_total(grad_total, left_side, right_side):
    return grad_total


def body(llm_grad, slot_row, counts, saved_in, saved_pre, weights, channel_scale):
    sections = lax.axis_size("pipe")
    section_index = lax.axis_index("pipe")
    micro_count = llm_grad.shape[0]
    row_count = llm_grad.shape[1]
    model_width = llm_grad.shape[2]
    hidden = saved_pre.shape[3]
    is_up = section_index % 2 == 0
    is_top = section_index == sections - 1
    full_weight = lax.all_gather(weights[0], "dp", axis=0, tiled=True)
    channel_gain = channel_scale[0]
    top_grad = local_top(llm_grad, slot_row[:, 0], counts[0])
    zero_wide = jnp.zeros((row_count, model_width), jnp.float32)
    zero_narrow = jnp.zeros((row_count, model_width), jnp.bfloat16)
    zero_hidden = jnp.zeros((row_count, hidden), jnp.bfloat16)

    def spare_work(incoming, hidden_in, inputs, pre_act):
        return (zero_wide, zero_hidden, zero_narrow, zero_hidden)

    def down_work(incoming, hidden_in, inputs, pre_act):
        scaled = (incoming.astype(jnp.float32) * channel_gain).astype(jnp.bfloat16)
        hidden_grad = jnp.dot(scaled, full_weight, preferred_element_type=jnp.float32).astype(
            jnp.bfloat16
        )
        activated = gelu_parts(pre_act.astype(jnp.float32))[0].astype(jnp.bfloat16)
        return (zero_wide, hidden_grad, scaled, activated)

    def up_work(incoming, hidden_in, inputs, pre_act):
        act_grad = (
            hidden_in.astype(jnp.float32) * gelu_parts(pre_act.astype(jnp.float32))[1]
        ).astype(jnp.bfloat16)
        values = inputs.astype(jnp.float32)
        center = values - jnp.mean(values, axis=-1, keepdims=True)
        inv_std = lax.rsqrt(jnp.mean(center * center, axis=-1, keepdims=True) + norm_eps)
        normed = (center * inv_std * channel_gain).astype(jnp.bfloat16)
        partial_value = lax.dot_general(
            act_grad, full_weight, (((1,), (1,)), ((), ())), preferred_element_type=jnp.float32
        )
        return (partial_value, zero_hidden, normed, act_grad)

    def advance(loop_state, tick_index):
        grad_store, out_buffer, recv_hidden, recv_res = loop_state
        micro_index = tick_index - (sections - 1 - section_index)
        is_valid = (micro_index >= 0) & (micro_index < micro_count)
        micro_safe = jnp.clip(micro_index, 0, micro_count - 1)
        incoming = jnp.where(is_top, top_grad[micro_safe], recv_res)
        inputs = saved_in[0, micro_safe]
        pre_act = saved_pre[0, micro_safe]
        branch = jnp.where(is_valid, jnp.where(is_up, 2, 1), 0).astype(jnp.int32)
        partial_value, hidden_out, left_side, right_side = lax.switch(
            branch, [spare_work, down_work, up_work], incoming, recv_hidden, inputs, pre_act
        )
        values = inputs.astype(jnp.float32)
        center = values - jnp.mean(values, axis=-1, keepdims=True)
        inv_std = lax.rsqrt(jnp.mean(center * center, axis=-1, keepdims=True) + norm_eps)
        unit_rows = center * inv_std
        summed = jax.tree.map(
            lambda part: part.astype(jnp.float32), lax.psum(shortened(partial_value), "tensor")
        )
        back_out = norm_back(incoming, summed, unit_rows, inv_std, channel_gain)
        outgoing = jnp.where(is_up, back_out, incoming)
        write_at = jnp.where(is_valid, micro_safe, micro_count)
        out_buffer = lax.dynamic_update_index_in_dim(out_buffer, outgoing, write_at, 0)
        grad_store = lax.cond(is_valid, add_term, keep_total, grad_store, left_side, right_side)
        recv_hidden, recv_res = (
            shifted(shortened(hidden_out), "pipe", -1).astype(hidden_out.dtype),
            shifted(outgoing, "pipe", -1),
        )
        return ((grad_store, out_buffer, recv_hidden, recv_res), None)

    grad_store = jnp.zeros((model_width, hidden), jnp.float32)
    out_buffer = jnp.zeros((micro_count + 1, row_count, model_width), jnp.bfloat16)
    tick_count = micro_count + sections - 1
    loop_state = (grad_store, out_buffer, zero_hidden, zero_narrow)
    loop_state, unused = lax.scan(advance, loop_state, jnp.arange(tick_count, dtype=jnp.int32))
    grad_store, out_buffer, recv_hidden, recv_res = loop_state
    weight_out = lax.psum_scatter(
        grad_store.astype(jnp.bfloat16), "dp", scatter_dimension=0, tiled=True
    )
    return (weight_out[None], out_buffer[:micro_count][None])


def solution(mesh):
    in_specs = (
        P(None, "dp", None),
        P(None, "dp", None),
        P("dp", None),
        P("pipe", None, "dp", None),
        P("pipe", None, "dp", "tensor"),
        P("pipe", "dp", "tensor"),
        P("pipe", None),
    )
    out_specs = (P("pipe", "dp", "tensor"), P("pipe", None, "dp", None))
    return jax.shard_map(body, mesh=mesh, in_specs=in_specs, out_specs=out_specs, check_vma=False)
```

profile of v0, /device:TPU:160, one launch (start us, length us, event | category | flops | bytes accessed | tf_op | source)
XLA Modules:
  0.0 917.6 jit_solution(5709121995667591268)
XLA Ops:
  11.7 160.9 %all-gather.3.cloned.1.call-done = bf16[1,1664,3200]{2,0,1:T(2,128)(2,1)} async-done(((bf16[1,52,3200]{2,0,1:T(2,128)(2,1)}), bf16[1,1664,3200]{2,0,1:T(2,128)(2,1)}) %all-gather.3.cloned.1.call-update) | async-done | bytes 10649616 | tf_op jit(solution)/shard_map/all_gather | solution.py:70
  172.6 15.3 %copy.13 = bf16[1,1664,3200]{2,1,0:T(8,128)(2,1)} copy(bf16[1,1664,3200]{2,0,1:T(2,128)(2,1)} %all-gather.3.cloned.1.call-done) | data formatting | bytes 21299200
  188.0 8.4 broadcast_in_dim.59
  196.5 443.6 %while.21 = (s32[]{:T(128)}, f32[1664,3200]{1,0:T(8,128)}, bf16[5,32,1664]{2,1,0:T(8,128)(2,1)S(1)}, bf16[32,3200]{1,0:T(8,128)(2,1)S(1)}, bf16[32,1664]{1,0:T(8...) while((s32[]{:T(128)}, f32[1664,3200]{1,0:T(8,128)}, ...), condition=%wide.region_13.14_spmd, body=%wide.region_0.13_spmd.sunk | while | flops 690257984 | bytes 59273832 | solution.py:135
  203.5 32.2 %all-reduce.4.cloned.1.call-done = bf16[32,1664]{1,0:T(8,128)(2,1)} async-done(((bf16[32,1664]{1,0:T(8,128)(2,1)}), bf16[32,1664]{1,0:T(8,128)(2,1)}) %all-reduce.4.cloned.1.call-update) | async-done | bytes 106512 | tf_op jit(solution)/shard_map/while/body/eval_jaxpr/psum | solution.py:118
  251.8 47.5 %all-reduce.4.cloned.1.call-done = bf16[32,1664]{1,0:T(8,128)(2,1)} async-done(((bf16[32,1664]{1,0:T(8,128)(2,1)}), bf16[32,1664]{1,0:T(8,128)(2,1)}) %all-reduce.4.cloned.1.call-update) | async-done | bytes 106512 | tf_op jit(solution)/shard_map/while/body/eval_jaxpr/psum | solution.py:118
  315.4 49.2 %all-reduce.4.cloned.1.call-done = bf16[32,1664]{1,0:T(8,128)(2,1)} async-done(((bf16[32,1664]{1,0:T(8,128)(2,1)}), bf16[32,1664]{1,0:T(8,128)(2,1)}) %all-reduce.4.cloned.1.call-update) | async-done | bytes 106512 | tf_op jit(solution)/shard_map/while/body/eval_jaxpr/psum | solution.py:118
  377.1 9.3 %conditional.4 = (bf16[32,1664]{1,0:T(8,128)(2,1)S(1)}, bf16[32,3200]{1,0:T(8,128)(2,1)S(1)}, bf16[32,1664]{1,0:T(8,128)(2,1)}, bf16[32,3200]{1,0:T(8,128)(2,1)}) conditional(s32[]{:T(128)} %clamp.6, () %tuple.65, (bf16[32,1664]{1,0:T(8,128)(2,1)S(1)}, f32[1,1664]{1,0:T(1,128)S(1)}, bf16[1664,3200]{1,0:T(8,128)(2,1)}, ...), branch_computations={%region_1.1_spmd, %region_2.2_spmd, %region_3.5_spmd} | conditional | flops 342601760 | bytes 12227238 | solution.py:110
  379.2 7.2 fusion.36
  388.7 41.3 %all-reduce.4.cloned.1.call-done = bf16[32,1664]{1,0:T(8,128)(2,1)} async-done(((bf16[32,1664]{1,0:T(8,128)(2,1)}), bf16[32,1664]{1,0:T(8,128)(2,1)}) %all-reduce.4.cloned.1.call-update) | async-done | bytes 106512 | tf_op jit(solution)/shard_map/while/body/eval_jaxpr/psum | solution.py:118
  433.5 17.3 %conditional.5 = (f32[1664,3200]{1,0:T(8,128)}) conditional(s32[]{:T(128)} %convert_element_type.179, f32[1664,3200]{1,0:T(8,128)} %get-tuple-element.404, (bf16[32,1664]{1,0:T(8,128)(2,1)}, bf16[32,3200]{1,0:T(8,128)(2,1)}, f32[1664,3200]{1,0:T(8,128)}) %tuple.68), branch_computations={%region_6.6_spmd, %region_7.7_spmd} | conditional | flops 346112000 | bytes 42909704 | solution.py:124
  433.5 17.3 %convolution_add_fusion = f32[1664,3200]{1,0:T(8,128)} fusion(f32[1664,3200]{1,0:T(8,128)} %get-tuple-element.188, bf16[32,1664]{1,0:T(8,128)(2,1)} %get-tuple-element.189, bf16[32,3200]{1,0:T(8,128)(2,1)} %get-tuple-element.190), kind=kOutput, calls=%fused_computation | convolution fusion | flops 346112000 | bytes 42909696 | tf_op jit(solution)/shard_map/while/body/eval_jaxpr/cond/branch_1_fun/dot_general | solution.py:52
  454.1 9.3 %conditional.4 = (bf16[32,1664]{1,0:T(8,128)(2,1)S(1)}, bf16[32,3200]{1,0:T(8,128)(2,1)S(1)}, bf16[32,1664]{1,0:T(8,128)(2,1)}, bf16[32,3200]{1,0:T(8,128)(2,1)}) conditional(s32[]{:T(128)} %clamp.6, () %tuple.65, (bf16[32,1664]{1,0:T(8,128)(2,1)S(1)}, f32[1,1664]{1,0:T(1,128)S(1)}, bf16[1664,3200]{1,0:T(8,128)(2,1)}, ...), branch_computations={%region_1.1_spmd, %region_2.2_spmd, %region_3.5_spmd} | conditional | flops 342601760 | bytes 12227238 | solution.py:110
  465.7 29.7 %all-reduce.4.cloned.1.call-done = bf16[32,1664]{1,0:T(8,128)(2,1)} async-done(((bf16[32,1664]{1,0:T(8,128)(2,1)}), bf16[32,1664]{1,0:T(8,128)(2,1)}) %all-reduce.4.cloned.1.call-update) | async-done | bytes 106512 | tf_op jit(solution)/shard_map/while/body/eval_jaxpr/psum | solution.py:118
  498.9 17.3 %conditional.5 = (f32[1664,3200]{1,0:T(8,128)}) conditional(s32[]{:T(128)} %convert_element_type.179, f32[1664,3200]{1,0:T(8,128)} %get-tuple-element.404, (bf16[32,1664]{1,0:T(8,128)(2,1)}, bf16[32,3200]{1,0:T(8,128)(2,1)}, f32[1664,3200]{1,0:T(8,128)}) %tuple.68), branch_computations={%region_6.6_spmd, %region_7.7_spmd} | conditional | flops 346112000 | bytes 42909704 | solution.py:124
  498.9 17.3 %convolution_add_fusion = f32[1664,3200]{1,0:T(8,128)} fusion(f32[1664,3200]{1,0:T(8,128)} %get-tuple-element.188, bf16[32,1664]{1,0:T(8,128)(2,1)} %get-tuple-element.189, bf16[32,3200]{1,0:T(8,128)(2,1)} %get-tuple-element.190), kind=kOutput, calls=%fused_computation | convolution fusion | flops 346112000 | bytes 42909696 | tf_op jit(solution)/shard_map/while/body/eval_jaxpr/cond/branch_1_fun/dot_general | solution.py:52
  519.5 9.3 %conditional.4 = (bf16[32,1664]{1,0:T(8,128)(2,1)S(1)}, bf16[32,3200]{1,0:T(8,128)(2,1)S(1)}, bf16[32,1664]{1,0:T(8,128)(2,1)}, bf16[32,3200]{1,0:T(8,128)(2,1)}) conditional(s32[]{:T(128)} %clamp.6, () %tuple.65, (bf16[32,1664]{1,0:T(8,128)(2,1)S(1)}, f32[1,1664]{1,0:T(1,128)S(1)}, bf16[1664,3200]{1,0:T(8,128)(2,1)}, ...), branch_computations={%region_1.1_spmd, %region_2.2_spmd, %region_3.5_spmd} | conditional | flops 342601760 | bytes 12227238 | solution.py:110
  521.5 7.2 fusion.36
  531.1 26.4 %all-reduce.4.cloned.1.call-done = bf16[32,1664]{1,0:T(8,128)(2,1)} async-done(((bf16[32,1664]{1,0:T(8,128)(2,1)}), bf16[32,1664]{1,0:T(8,128)(2,1)}) %all-reduce.4.cloned.1.call-update) | async-done | bytes 106512 | tf_op jit(solution)/shard_map/while/body/eval_jaxpr/psum | solution.py:118
  561.0 17.3 %conditional.5 = (f32[1664,3200]{1,0:T(8,128)}) conditional(s32[]{:T(128)} %convert_element_type.179, f32[1664,3200]{1,0:T(8,128)} %get-tuple-element.404, (bf16[32,1664]{1,0:T(8,128)(2,1)}, bf16[32,3200]{1,0:T(8,128)(2,1)}, f32[1664,3200]{1,0:T(8,128)}) %tuple.68), branch_computations={%region_6.6_spmd, %region_7.7_spmd} | conditional | flops 346112000 | bytes 42909704 | solution.py:124
  561.0 17.3 %convolution_add_fusion = f32[1664,3200]{1,0:T(8,128)} fusion(f32[1664,3200]{1,0:T(8,128)} %get-tuple-element.188, bf16[32,1664]{1,0:T(8,128)(2,1)} %get-tuple-element.189, bf16[32,3200]{1,0:T(8,128)(2,1)} %get-tuple-element.190), kind=kOutput, calls=%fused_computation | convolution fusion | flops 346112000 | bytes 42909696 | tf_op jit(solution)/shard_map/while/body/eval_jaxpr/cond/branch_1_fun/dot_general | solution.py:52
  581.6 9.3 %conditional.4 = (bf16[32,1664]{1,0:T(8,128)(2,1)S(1)}, bf16[32,3200]{1,0:T(8,128)(2,1)S(1)}, bf16[32,1664]{1,0:T(8,128)(2,1)}, bf16[32,3200]{1,0:T(8,128)(2,1)}) conditional(s32[]{:T(128)} %clamp.6, () %tuple.65, (bf16[32,1664]{1,0:T(8,128)(2,1)S(1)}, f32[1,1664]{1,0:T(1,128)S(1)}, bf16[1664,3200]{1,0:T(8,128)(2,1)}, ...), branch_computations={%region_1.1_spmd, %region_2.2_spmd, %region_3.5_spmd} | conditional | flops 342601760 | bytes 12227238 | solution.py:110
  583.6 7.2 fusion.36
  593.1 26.1 %all-reduce.4.cloned.1.call-done = bf16[32,1664]{1,0:T(8,128)(2,1)} async-done(((bf16[32,1664]{1,0:T(8,128)(2,1)}), bf16[32,1664]{1,0:T(8,128)(2,1)}) %all-reduce.4.cloned.1.call-update) | async-done | bytes 106512 | tf_op jit(solution)/shard_map/while/body/eval_jaxpr/psum | solution.py:118
  622.7 17.3 %conditional.5 = (f32[1664,3200]{1,0:T(8,128)}) conditional(s32[]{:T(128)} %convert_element_type.179, f32[1664,3200]{1,0:T(8,128)} %get-tuple-element.404, (bf16[32,1664]{1,0:T(8,128)(2,1)}, bf16[32,3200]{1,0:T(8,128)(2,1)}, f32[1664,3200]{1,0:T(8,128)}) %tuple.68), branch_computations={%region_6.6_spmd, %region_7.7_spmd} | conditional | flops 346112000 | bytes 42909704 | solution.py:124
  622.8 17.3 %convolution_add_fusion = f32[1664,3200]{1,0:T(8,128)} fusion(f32[1664,3200]{1,0:T(8,128)} %get-tuple-element.188, bf16[32,1664]{1,0:T(8,128)(2,1)} %get-tuple-element.189, bf16[32,3200]{1,0:T(8,128)(2,1)} %get-tuple-element.190), kind=kOutput, calls=%fused_computation | convolution fusion | flops 346112000 | bytes 42909696 | tf_op jit(solution)/shard_map/while/body/eval_jaxpr/cond/branch_1_fun/dot_general | solution.py:52
  640.1 12.3 %convert_element_type.68 = bf16[1664,3200]{1,0:T(8,128)(2,1)} convert(f32[1664,3200]{1,0:T(8,128)} %get-tuple-element.215) | non-fusion elementwise | flops 5324800 | bytes 31948800 | tf_op jit(solution)/shard_map/convert_element_type | solution.py:138
  652.4 150.3 %fusion = bf16[64,3200]{1,0:T(8,128)(2,1)S(1)} fusion(bf16[1664,3200]{1,0:T(8,128)(2,1)} %convert_element_type.68), kind=kCustom, calls=%all-reduce-scatter | all-reduce-scatter fusion | flops 6553601 | bytes 11060224
  817.5 11.5 %collective-permute-done.7 = bf16[52,3200]{1,0:T(8,128)(2,1)S(1)} collective-permute-done((bf16[52,3200]{1,0:T(8,128)(2,1)S(1)}, bf16[52,3200]{1,0:T(8,128)(2,1)S(1)}, u32[]{:S(2)}, u32[]{:S(2)}) %collective-permute-start.7) | collective-permute-done | bytes 332832
  831.7 7.9 collective-permute-done.2
  842.7 46.2 %collective-permute-done.6 = bf16[64,3200]{1,0:T(8,128)(2,1)} collective-permute-done((bf16[64,3200]{1,0:T(8,128)(2,1)S(1)}, bf16[64,3200]{1,0:T(8,128)(2,1)}, u32[]{:S(2)}, u32[]{:S(2)}) %collective-permute-start.6) | collective-permute-done | bytes 409632
  888.8 21.1 %concatenate = bf16[436,3200]{1,0:T(8,128)(2,1)S(1)} concatenate(bf16[52,3200]{1,0:T(8,128)(2,1)} %copy-done.6, bf16[64,3200]{1,0:T(8,128)(2,1)} %collective-permute-done.6, bf16[64,3200]{1,0:T(8,128)(2,1)} %copy-done.5, bf16[64,3200]{1,0:T(8,128)(2,1)} %copy-done.4, bf16[64,3200]{1,0:T(8,128)(2,1)} %copy-done.3, bf16[64,3200]{1,0:T(8,128)(2,1)} %copy-done.2, ...), dimensions={0} | concatenate | bytes 5580800
  (220 shorter events, 124.1 us)
Async XLA Ops:
  7.2 165.5 %all-gather.3.cloned.1.call-start = ((), (), s32[]{:S(2)}) async-start(), calls=%async_computation | async-start | bytes 21964800 | tf_op jit(solution)/shard_map/all_gather | solution.py:70
  188.0 8.5 copy-start.1
  196.5 39.1 %all-reduce.4.cloned.1.call-start = ((), (), s32[]{:S(2)}) async-start(), calls=%async_computation.1 | async-start | bytes 212992 | tf_op jit(solution)/shard_map/while/body/eval_jaxpr/psum | solution.py:118
  201.9 37.2 %collective-permute-start = (bf16[32,3200]{1,0:T(8,128)(2,1)S(1)}, bf16[32,3200]{1,0:T(8,128)(2,1)S(1)}, u32[]{:S(2)}, u32[]{:S(2)}) collective-permute-start(bf16[32,3200]{1,0:T(8,128)(2,1)S(1)} %get-tuple-element.368), channel_id=1, source_target_pairs={{64,0},{128,64},{192,128},{65,1},{129,65},{193,129},{66,2},{130,66... | collective-permute-start | bytes 614408 | tf_op jit(solution)/shard_map/while/body/eval_jaxpr/ppermute | solution.py:22
  237.8 7.1 collective-permute-start.1
  244.9 54.4 %all-reduce.4.cloned.1.call-start = ((), (), s32[]{:S(2)}) async-start(), calls=%async_computation.1 | async-start | bytes 212992 | tf_op jit(solution)/shard_map/while/body/eval_jaxpr/psum | solution.py:118
  250.2 52.5 %collective-permute-start = (bf16[32,3200]{1,0:T(8,128)(2,1)S(1)}, bf16[32,3200]{1,0:T(8,128)(2,1)S(1)}, u32[]{:S(2)}, u32[]{:S(2)}) collective-permute-start(bf16[32,3200]{1,0:T(8,128)(2,1)S(1)} %get-tuple-element.368), channel_id=1, source_target_pairs={{64,0},{128,64},{192,128},{65,1},{129,65},{193,129},{66,2},{130,66... | collective-permute-start | bytes 614408 | tf_op jit(solution)/shard_map/while/body/eval_jaxpr/ppermute | solution.py:22
  301.4 7.1 collective-permute-start.1
  308.5 56.1 %all-reduce.4.cloned.1.call-start = ((), (), s32[]{:S(2)}) async-start(), calls=%async_computation.1 | async-start | bytes 212992 | tf_op jit(solution)/shard_map/while/body/eval_jaxpr/psum | solution.py:118
  313.9 54.3 %collective-permute-start = (bf16[32,3200]{1,0:T(8,128)(2,1)S(1)}, bf16[32,3200]{1,0:T(8,128)(2,1)S(1)}, u32[]{:S(2)}, u32[]{:S(2)}) collective-permute-start(bf16[32,3200]{1,0:T(8,128)(2,1)S(1)} %get-tuple-element.368), channel_id=1, source_target_pairs={{64,0},{128,64},{192,128},{65,1},{129,65},{193,129},{66,2},{130,66... | collective-permute-start | bytes 614408 | tf_op jit(solution)/shard_map/while/body/eval_jaxpr/ppermute | solution.py:22
  366.8 7.1 collective-permute-start.1
  373.9 56.1 %all-reduce.4.cloned.1.call-start = ((), (), s32[]{:S(2)}) async-start(), calls=%async_computation.1 | async-start | bytes 212992 | tf_op jit(solution)/shard_map/while/body/eval_jaxpr/psum | solution.py:118
  387.2 63.6 %collective-permute-start = (bf16[32,3200]{1,0:T(8,128)(2,1)S(1)}, bf16[32,3200]{1,0:T(8,128)(2,1)S(1)}, u32[]{:S(2)}, u32[]{:S(2)}) collective-permute-start(bf16[32,3200]{1,0:T(8,128)(2,1)S(1)} %get-tuple-element.368), channel_id=1, source_target_pairs={{64,0},{128,64},{192,128},{65,1},{129,65},{193,129},{66,2},{130,66... | collective-permute-start | bytes 614408 | tf_op jit(solution)/shard_map/while/body/eval_jaxpr/ppermute | solution.py:22
  432.2 18.6 %collective-permute-start.1 = (bf16[32,1664]{1,0:T(8,128)(2,1)S(1)}, bf16[32,1664]{1,0:T(8,128)(2,1)S(1)}, u32[]{:S(2)}, u32[]{:S(2)}) collective-permute-start(bf16[32,1664]{1,0:T(8,128)(2,1)S(1)} %get-tuple-element.369), channel_id=1, source_target_pairs={{64,0},{128,64},{192,128},{65,1},{129,65},{193,129},{66,2},{130,66... | collective-permute-start | bytes 319496 | tf_op jit(solution)/shard_map/while/body/eval_jaxpr/ppermute | solution.py:22
  450.8 44.6 %all-reduce.4.cloned.1.call-start = ((), (), s32[]{:S(2)}) async-start(), calls=%async_computation.1 | async-start | bytes 212992 | tf_op jit(solution)/shard_map/while/body/eval_jaxpr/psum | solution.py:118
  464.1 52.1 %collective-permute-start = (bf16[32,3200]{1,0:T(8,128)(2,1)S(1)}, bf16[32,3200]{1,0:T(8,128)(2,1)S(1)}, u32[]{:S(2)}, u32[]{:S(2)}) collective-permute-start(bf16[32,3200]{1,0:T(8,128)(2,1)S(1)} %get-tuple-element.368), channel_id=1, source_target_pairs={{64,0},{128,64},{192,128},{65,1},{129,65},{193,129},{66,2},{130,66... | collective-permute-start | bytes 614408 | tf_op jit(solution)/shard_map/while/body/eval_jaxpr/ppermute | solution.py:22
  497.6 18.6 %collective-permute-start.1 = (bf16[32,1664]{1,0:T(8,128)(2,1)S(1)}, bf16[32,1664]{1,0:T(8,128)(2,1)S(1)}, u32[]{:S(2)}, u32[]{:S(2)}) collective-permute-start(bf16[32,1664]{1,0:T(8,128)(2,1)S(1)} %get-tuple-element.369), channel_id=1, source_target_pairs={{64,0},{128,64},{192,128},{65,1},{129,65},{193,129},{66,2},{130,66... | collective-permute-start | bytes 319496 | tf_op jit(solution)/shard_map/while/body/eval_jaxpr/ppermute | solution.py:22
  516.2 41.3 %all-reduce.4.cloned.1.call-start = ((), (), s32[]{:S(2)}) async-start(), calls=%async_computation.1 | async-start | bytes 212992 | tf_op jit(solution)/shard_map/while/body/eval_jaxpr/psum | solution.py:118
  529.5 48.7 %collective-permute-start = (bf16[32,3200]{1,0:T(8,128)(2,1)S(1)}, bf16[32,3200]{1,0:T(8,128)(2,1)S(1)}, u32[]{:S(2)}, u32[]{:S(2)}) collective-permute-start(bf16[32,3200]{1,0:T(8,128)(2,1)S(1)} %get-tuple-element.368), channel_id=1, source_target_pairs={{64,0},{128,64},{192,128},{65,1},{129,65},{193,129},{66,2},{130,66... | collective-permute-start | bytes 614408 | tf_op jit(solution)/shard_map/while/body/eval_jaxpr/ppermute | solution.py:22
  559.7 18.6 %collective-permute-start.1 = (bf16[32,1664]{1,0:T(8,128)(2,1)S(1)}, bf16[32,1664]{1,0:T(8,128)(2,1)S(1)}, u32[]{:S(2)}, u32[]{:S(2)}) collective-permute-start(bf16[32,1664]{1,0:T(8,128)(2,1)S(1)} %get-tuple-element.369), channel_id=1, source_target_pairs={{64,0},{128,64},{192,128},{65,1},{129,65},{193,129},{66,2},{130,66... | collective-permute-start | bytes 319496 | tf_op jit(solution)/shard_map/while/body/eval_jaxpr/ppermute | solution.py:22
  578.3 41.0 %all-reduce.4.cloned.1.call-start = ((), (), s32[]{:S(2)}) async-start(), calls=%async_computation.1 | async-start | bytes 212992 | tf_op jit(solution)/shard_map/while/body/eval_jaxpr/psum | solution.py:118
  591.6 48.5 %collective-permute-start = (bf16[32,3200]{1,0:T(8,128)(2,1)S(1)}, bf16[32,3200]{1,0:T(8,128)(2,1)S(1)}, u32[]{:S(2)}, u32[]{:S(2)}) collective-permute-start(bf16[32,3200]{1,0:T(8,128)(2,1)S(1)} %get-tuple-element.368), channel_id=1, source_target_pairs={{64,0},{128,64},{192,128},{65,1},{129,65},{193,129},{66,2},{130,66... | collective-permute-start | bytes 614408 | tf_op jit(solution)/shard_map/while/body/eval_jaxpr/ppermute | solution.py:22
  621.4 18.6 %collective-permute-start.1 = (bf16[32,1664]{1,0:T(8,128)(2,1)S(1)}, bf16[32,1664]{1,0:T(8,128)(2,1)S(1)}, u32[]{:S(2)}, u32[]{:S(2)}) collective-permute-start(bf16[32,1664]{1,0:T(8,128)(2,1)S(1)} %get-tuple-element.369), channel_id=1, source_target_pairs={{64,0},{128,64},{192,128},{65,1},{129,65},{193,129},{66,2},{130,66... | collective-permute-start | bytes 319496 | tf_op jit(solution)/shard_map/while/body/eval_jaxpr/ppermute | solution.py:22
  640.1 164.7 %copy-start.7 = (u32[256]{0:T(256)S(1)}, u32[256]{0:T(256)}, u32[]{:S(2)}) copy-start(u32[256]{0:T(256)} %constant.123) | copy-start | bytes 3076
  802.8 26.2 %collective-permute-start.7 = (bf16[52,3200]{1,0:T(8,128)(2,1)S(1)}, bf16[52,3200]{1,0:T(8,128)(2,1)S(1)}, u32[]{:S(2)}, u32[]{:S(2)}) collective-permute-start(bf16[52,3200]{1,0:T(8,128)(2,1)S(1)} %slice.4), channel_id=1, source_target_pairs={{0,12},{2,14},{4,16},{6,18},{8,20},{10,22},{12,24},{14,26},{16,28}... | collective-permute-start | bytes 998408
  806.0 33.6 %collective-permute-start.2 = (bf16[64,3200]{1,0:T(8,128)(2,1)S(1)}, bf16[64,3200]{1,0:T(8,128)(2,1)S(1)}, u32[]{:S(2)}, u32[]{:S(2)}) collective-permute-start(bf16[64,3200]{1,0:T(8,128)(2,1)S(1)} %fusion), channel_id=1, source_target_pairs={{0,2},{2,4},{4,6},{6,8},{8,10},{10,12},{12,14},{14,16},{16,18},{18... | collective-permute-start | bytes 1228808
  807.9 33.1 %collective-permute-start.3 = (bf16[64,3200]{1,0:T(8,128)(2,1)S(1)}, bf16[64,3200]{1,0:T(8,128)(2,1)S(1)}, u32[]{:S(2)}, u32[]{:S(2)}) collective-permute-start(bf16[64,3200]{1,0:T(8,128)(2,1)S(1)} %fusion), channel_id=1, source_target_pairs={{0,4},{2,6},{4,8},{6,10},{8,12},{10,14},{12,16},{14,18},{16,20},{1... | collective-permute-start | bytes 1228808
  813.7 27.3 %collective-permute-start.4 = (bf16[64,3200]{1,0:T(8,128)(2,1)S(1)}, bf16[64,3200]{1,0:T(8,128)(2,1)S(1)}, u32[]{:S(2)}, u32[]{:S(2)}) collective-permute-start(bf16[64,3200]{1,0:T(8,128)(2,1)S(1)} %fusion), channel_id=1, source_target_pairs={{0,6},{2,8},{4,10},{6,12},{8,14},{10,16},{12,18},{14,20},{16,22},{... | collective-permute-start | bytes 1228808
  815.6 25.4 %collective-permute-start.5 = (bf16[64,3200]{1,0:T(8,128)(2,1)S(1)}, bf16[64,3200]{1,0:T(8,128)(2,1)S(1)}, u32[]{:S(2)}, u32[]{:S(2)}) collective-permute-start(bf16[64,3200]{1,0:T(8,128)(2,1)S(1)} %fusion), channel_id=1, source_target_pairs={{0,8},{2,10},{4,12},{6,14},{8,16},{10,18},{12,20},{14,22},{16,24},... | collective-permute-start | bytes 1228808
  829.0 12.0 %copy-start.6 = (bf16[52,3200]{1,0:T(8,128)(2,1)}, bf16[52,3200]{1,0:T(8,128)(2,1)S(1)}, u32[]{:S(2)}) copy-start(bf16[52,3200]{1,0:T(8,128)(2,1)S(1)} %collective-permute-done.7) | copy-start | bytes 998404
  829.0 59.8 %collective-permute-start.6 = (bf16[64,3200]{1,0:T(8,128)(2,1)S(1)}, bf16[64,3200]{1,0:T(8,128)(2,1)}, u32[]{:S(2)}, u32[]{:S(2)}) collective-permute-start(bf16[64,3200]{1,0:T(8,128)(2,1)S(1)} %fusion), channel_id=1, source_target_pairs={{0,10},{2,12},{4,14},{6,16},{8,18},{10,20},{12,22},{14,24},{16,26}... | collective-permute-start | bytes 1228808
  839.6 1.4 copy-start.2
  (10 other events, 7.0 us)
Sparse Core Ops, SparseCore 0:
  10.6 161.9 all-gather.2
  202.0 33.5 all-reduce.3
  250.4 48.8 all-reduce.3
  314.0 50.5 all-reduce.3
  387.3 42.6 all-reduce.3
  464.3 31.0 all-reduce.3
  529.6 27.7 all-reduce.3
  591.7 27.4 all-reduce.3
where the time goes:
time: 920 us; the launch traced here: 918 us
  waiting for transfers between devices  498 us (54%)
  blocking collectives  150 us (16%)
  matrix products  99.5 us (11%)
  local copies, waits for them, and re-layouts  70.8 us (8%)
  other arithmetic  45.2 us (5%)
  starting transfers between devices  33.6 us (4%)
  between operations  14.8 us (2%)
    psum x7, waiting for transfers between devices, advance(): lax.psum(shortened(partial_value), 'tensor')  252 us
    all_gather x1, waiting for transfers between devices, body(): full_weight = lax.all_gather(weights[0], 'dp', axis=0, tiled=True)  161 us
    unnamed x1, blocking collectives  150 us
    dot_general x4, matrix products, add_term(): lax.dot_general(left_side, right_side, (((0,), (0,)), ((), ())), preferre...  69.1 us
    unnamed x7, waiting for transfers between devices  66.9 us
    unnamed x19, local copies, waits for them, and re-layouts  41.1 us
    dot_general x4, matrix products, up_work(): lax.dot_general(act_grad, full_weight, (((1,), (1,)), ((), ())), preferre...  29 us
  transfers between devices with their start and end apart: 28, of which 15 were waited for; matrix products, arithmetic and copies ran while one was open for 10% of the time, Pallas kernels for 0%

commit v1 on v0

--- a/solution.py
+++ b/solution.py
@@ -67,7 +67,11 @@
     hidden = saved_pre.shape[3]
     is_up = section_index % 2 == 0
     is_top = section_index == sections - 1
-    full_weight = lax.all_gather(weights[0], "dp", axis=0, tiled=True)
+    block_2 = weights[0]
+    n_dev = lax.axis_size("dp")
+    blocks = jnp.stack([block_2 for _ in range(n_dev)])
+    blocks = lax.all_to_all(blocks, "dp", split_axis=0, concat_axis=0)
+    full_weight = jnp.concatenate(blocks, axis=0)
     channel_gain = channel_scale[0]
     top_grad = local_top(llm_grad, slot_row[:, 0], counts[0])
     zero_wide = jnp.zeros((row_count, model_width), jnp.float32)

time: 920 us -> 1040 us (1.13)
  waiting for transfers between devices: 498 us -> 607 us
    all_to_all x0 -> x1, waiting for transfers between devices: none -> 263 us  [body(): blocks = lax.all_to_all(blocks, 'dp', split_axis=0, concat_axis=0)]
    all_gather x1 -> x0, waiting for transfers between devices: 161 us -> none  [body(): full_weight = lax.all_gather(weights[0], 'dp', axis=0, tiled=True)]
    unnamed x19 -> x23, local copies, waits for them, and re-layouts: 41.1 us -> 23.4 us
    reshape x0 -> x1, local copies, waits for them, and re-layouts: none -> 13.9 us  [body(): full_weight = jnp.concatenate(blocks, axis=0)]
    unnamed x7 -> x6, waiting for transfers between devices: 66.9 us -> 66.9 us
  transfers between devices with their start and end apart: 28 -> 28, of which waited for: 15 -> 15; matrix products, arithmetic and copies ran while one was open for 10% -> 8% of each run, Pallas kernels for 0% -> 0%
where the time goes in v1:
time: 1040 us
  waiting for transfers between devices  607 us (58%)
  blocking collectives  150 us (14%)
  matrix products  98.4 us (9%)
  local copies, waits for them, and re-layouts  72.9 us (7%)
  other arithmetic  44.5 us (4%)
  starting transfers between devices  43.2 us (4%)
  between operations  14.8 us (1%)
    all_to_all x1, waiting for transfers between devices, body(): blocks = lax.all_to_all(blocks, 'dp', split_axis=0, concat_axis=0)  263 us
    psum x7, waiting for transfers between devices, advance(): lax.psum(shortened(partial_value), 'tensor')  260 us
    unnamed x1, blocking collectives  150 us
    dot_general x4, matrix products, add_term(): lax.dot_general(left_side, right_side, (((0,), (0,)), ((), ())), preferre...  69.2 us
    unnamed x6, waiting for transfers between devices  66.9 us
    dot_general x4, matrix products, up_work(): lax.dot_general(act_grad, full_weight, (((1,), (1,)), ((), ())), preferre...  29 us
    unnamed x23, local copies, waits for them, and re-layouts  23.4 us
  transfers between devices with their start and end apart: 28, of which 15 were waited for; matrix products, arithmetic and copies ran while one was open for 8% of the time, Pallas kernels for 0%

profile of v1, /device:TPU:160, one launch (start us, length us, event | category | flops | bytes accessed | tf_op | source)
XLA Modules:
  0.0 1037.5 jit_solution(8685593403046089057)
XLA Ops:
  13.1 9.6 all-to-all-start
  23.1 263.4 %all-to-all-done = bf16[32,52,3200]{2,1,0:T(8,128)(2,1)} async-done(((bf16[32,52,3200]{2,1,0:T(8,128)(2,1)}), bf16[32,52,3200]{2,1,0:T(8,128)(2,1)}, u32[]{:S(2)}, u32[]{:S(2)}) %all-to-all-start) | async-done | bytes 10649632 | tf_op jit(solution)/shard_map/all_to_all | solution.py:73
  286.5 13.9 %reshape.69 = bf16[1664,3200]{1,0:T(8,128)(2,1)} reshape(bf16[32,52,3200]{2,1,0:T(8,128)(2,1)} %all-to-all-done) | data formatting | bytes 21299200 | tf_op jit(solution)/shard_map/reshape | solution.py:74
  300.4 8.4 broadcast_in_dim.59
  309.0 450.9 %while.21 = (s32[]{:T(128)}, f32[1664,3200]{1,0:T(8,128)}, bf16[5,32,1664]{2,1,0:T(8,128)(2,1)S(1)}, bf16[32,3200]{1,0:T(8,128)(2,1)S(1)}, bf16[32,1664]{1,0:T(8...) while((s32[]{:T(128)}, f32[1664,3200]{1,0:T(8,128)}, ...), condition=%wide.region_13.14_spmd, body=%wide.region_0.13_spmd.sunk | while | flops 690257984 | bytes 59273832 | solution.py:139
  315.9 39.5 %all-reduce.4.cloned.1.call-done = bf16[32,1664]{1,0:T(8,128)(2,1)} async-done(((bf16[32,1664]{1,0:T(8,128)(2,1)}), bf16[32,1664]{1,0:T(8,128)(2,1)}) %all-reduce.4.cloned.1.call-update) | async-done | bytes 106512 | tf_op jit(solution)/shard_map/while/body/eval_jaxpr/psum | solution.py:122
  371.6 47.5 %all-reduce.4.cloned.1.call-done = bf16[32,1664]{1,0:T(8,128)(2,1)} async-done(((bf16[32,1664]{1,0:T(8,128)(2,1)}), bf16[32,1664]{1,0:T(8,128)(2,1)}) %all-reduce.4.cloned.1.call-update) | async-done | bytes 106512 | tf_op jit(solution)/shard_map/while/body/eval_jaxpr/psum | solution.py:122
  435.2 49.2 %all-reduce.4.cloned.1.call-done = bf16[32,1664]{1,0:T(8,128)(2,1)} async-done(((bf16[32,1664]{1,0:T(8,128)(2,1)}), bf16[32,1664]{1,0:T(8,128)(2,1)}) %all-reduce.4.cloned.1.call-update) | async-done | bytes 106512 | tf_op jit(solution)/shard_map/while/body/eval_jaxpr/psum | solution.py:122
  497.0 9.3 conditional.4
  499.0 7.2 fusion.36
  508.5 41.3 %all-reduce.4.cloned.1.call-done = bf16[32,1664]{1,0:T(8,128)(2,1)} async-done(((bf16[32,1664]{1,0:T(8,128)(2,1)}), bf16[32,1664]{1,0:T(8,128)(2,1)}) %all-reduce.4.cloned.1.call-update) | async-done | bytes 106512 | tf_op jit(solution)/shard_map/while/body/eval_jaxpr/psum | solution.py:122
  553.3 17.3 %conditional.5 = (f32[1664,3200]{1,0:T(8,128)}) conditional(s32[]{:T(128)} %convert_element_type.179, f32[1664,3200]{1,0:T(8,128)} %get-tuple-element.404, (bf16[32,1664]{1,0:T(8,128)(2,1)}, bf16[32,3200]{1,0:T(8,128)(2,1)}, f32[1664,3200]{1,0:T(8,128)}) %tuple.68), branch_computations={%region_6.6_spmd, %region_7.7_spmd} | conditional | flops 346112000 | bytes 42909704 | solution.py:128
  553.3 17.3 %convolution_add_fusion = f32[1664,3200]{1,0:T(8,128)} fusion(f32[1664,3200]{1,0:T(8,128)} %get-tuple-element.188, bf16[32,1664]{1,0:T(8,128)(2,1)} %get-tuple-element.189, bf16[32,3200]{1,0:T(8,128)(2,1)} %get-tuple-element.190), kind=kOutput, calls=%fused_computation | convolution fusion | flops 346112000 | bytes 42909696 | tf_op jit(solution)/shard_map/while/body/eval_jaxpr/cond/branch_1_fun/dot_general | solution.py:52
  573.9 9.3 conditional.4
  585.5 29.7 %all-reduce.4.cloned.1.call-done = bf16[32,1664]{1,0:T(8,128)(2,1)} async-done(((bf16[32,1664]{1,0:T(8,128)(2,1)}), bf16[32,1664]{1,0:T(8,128)(2,1)}) %all-reduce.4.cloned.1.call-update) | async-done | bytes 106512 | tf_op jit(solution)/shard_map/while/body/eval_jaxpr/psum | solution.py:122
  618.7 17.3 %conditional.5 = (f32[1664,3200]{1,0:T(8,128)}) conditional(s32[]{:T(128)} %convert_element_type.179, f32[1664,3200]{1,0:T(8,128)} %get-tuple-element.404, (bf16[32,1664]{1,0:T(8,128)(2,1)}, bf16[32,3200]{1,0:T(8,128)(2,1)}, f32[1664,3200]{1,0:T(8,128)}) %tuple.68), branch_computations={%region_6.6_spmd, %region_7.7_spmd} | conditional | flops 346112000 | bytes 42909704 | solution.py:128
  618.7 17.3 %convolution_add_fusion = f32[1664,3200]{1,0:T(8,128)} fusion(f32[1664,3200]{1,0:T(8,128)} %get-tuple-element.188, bf16[32,1664]{1,0:T(8,128)(2,1)} %get-tuple-element.189, bf16[32,3200]{1,0:T(8,128)(2,1)} %get-tuple-element.190), kind=kOutput, calls=%fused_computation | convolution fusion | flops 346112000 | bytes 42909696 | tf_op jit(solution)/shard_map/while/body/eval_jaxpr/cond/branch_1_fun/dot_general | solution.py:52
  639.3 9.3 conditional.4
  650.9 26.4 %all-reduce.4.cloned.1.call-done = bf16[32,1664]{1,0:T(8,128)(2,1)} async-done(((bf16[32,1664]{1,0:T(8,128)(2,1)}), bf16[32,1664]{1,0:T(8,128)(2,1)}) %all-reduce.4.cloned.1.call-update) | async-done | bytes 106512 | tf_op jit(solution)/shard_map/while/body/eval_jaxpr/psum | solution.py:122
  680.8 17.3 %conditional.5 = (f32[1664,3200]{1,0:T(8,128)}) conditional(s32[]{:T(128)} %convert_element_type.179, f32[1664,3200]{1,0:T(8,128)} %get-tuple-element.404, (bf16[32,1664]{1,0:T(8,128)(2,1)}, bf16[32,3200]{1,0:T(8,128)(2,1)}, f32[1664,3200]{1,0:T(8,128)}) %tuple.68), branch_computations={%region_6.6_spmd, %region_7.7_spmd} | conditional | flops 346112000 | bytes 42909704 | solution.py:128
  680.8 17.3 %convolution_add_fusion = f32[1664,3200]{1,0:T(8,128)} fusion(f32[1664,3200]{1,0:T(8,128)} %get-tuple-element.188, bf16[32,1664]{1,0:T(8,128)(2,1)} %get-tuple-element.189, bf16[32,3200]{1,0:T(8,128)(2,1)} %get-tuple-element.190), kind=kOutput, calls=%fused_computation | convolution fusion | flops 346112000 | bytes 42909696 | tf_op jit(solution)/shard_map/while/body/eval_jaxpr/cond/branch_1_fun/dot_general | solution.py:52
  701.4 9.3 conditional.4
  703.4 7.2 fusion.36
  712.9 26.1 %all-reduce.4.cloned.1.call-done = bf16[32,1664]{1,0:T(8,128)(2,1)} async-done(((bf16[32,1664]{1,0:T(8,128)(2,1)}), bf16[32,1664]{1,0:T(8,128)(2,1)}) %all-reduce.4.cloned.1.call-update) | async-done | bytes 106512 | tf_op jit(solution)/shard_map/while/body/eval_jaxpr/psum | solution.py:122
  742.5 17.3 %conditional.5 = (f32[1664,3200]{1,0:T(8,128)}) conditional(s32[]{:T(128)} %convert_element_type.179, f32[1664,3200]{1,0:T(8,128)} %get-tuple-element.404, (bf16[32,1664]{1,0:T(8,128)(2,1)}, bf16[32,3200]{1,0:T(8,128)(2,1)}, f32[1664,3200]{1,0:T(8,128)}) %tuple.68), branch_computations={%region_6.6_spmd, %region_7.7_spmd} | conditional | flops 346112000 | bytes 42909704 | solution.py:128
  742.5 17.3 %convolution_add_fusion = f32[1664,3200]{1,0:T(8,128)} fusion(f32[1664,3200]{1,0:T(8,128)} %get-tuple-element.188, bf16[32,1664]{1,0:T(8,128)(2,1)} %get-tuple-element.189, bf16[32,3200]{1,0:T(8,128)(2,1)} %get-tuple-element.190), kind=kOutput, calls=%fused_computation | convolution fusion | flops 346112000 | bytes 42909696 | tf_op jit(solution)/shard_map/while/body/eval_jaxpr/cond/branch_1_fun/dot_general | solution.py:52
  759.8 12.3 %convert_element_type.68 = bf16[1664,3200]{1,0:T(8,128)(2,1)} convert(f32[1664,3200]{1,0:T(8,128)} %get-tuple-element.215) | non-fusion elementwise | flops 5324800 | bytes 31948800 | tf_op jit(solution)/shard_map/convert_element_type | solution.py:142
  772.1 150.4 %fusion = bf16[64,3200]{1,0:T(8,128)(2,1)S(1)} fusion(bf16[1664,3200]{1,0:T(8,128)(2,1)} %convert_element_type.68), kind=kCustom, calls=%all-reduce-scatter | all-reduce-scatter fusion | flops 6553601 | bytes 11060224
  937.4 11.5 %collective-permute-done.7 = bf16[52,3200]{1,0:T(8,128)(2,1)S(1)} collective-permute-done((bf16[52,3200]{1,0:T(8,128)(2,1)S(1)}, bf16[52,3200]{1,0:T(8,128)(2,1)S(1)}, u32[]{:S(2)}, u32[]{:S(2)}) %collective-permute-start.7) | collective-permute-done | bytes 332832
  951.6 7.9 collective-permute-done.2
  962.5 46.2 %collective-permute-done.6 = bf16[64,3200]{1,0:T(8,128)(2,1)} collective-permute-done((bf16[64,3200]{1,0:T(8,128)(2,1)S(1)}, bf16[64,3200]{1,0:T(8,128)(2,1)}, u32[]{:S(2)}, u32[]{:S(2)}) %collective-permute-start.6) | collective-permute-done | bytes 409632
  1008.7 21.1 %concatenate = bf16[436,3200]{1,0:T(8,128)(2,1)S(1)} concatenate(bf16[52,3200]{1,0:T(8,128)(2,1)} %copy-done.7, bf16[64,3200]{1,0:T(8,128)(2,1)} %collective-permute-done.6, bf16[64,3200]{1,0:T(8,128)(2,1)} %copy-done.6, bf16[64,3200]{1,0:T(8,128)(2,1)} %copy-done.5, bf16[64,3200]{1,0:T(8,128)(2,1)} %copy-done.4, bf16[64,3200]{1,0:T(8,128)(2,1)} %copy-done.3, ...), dimensions={0} | concatenate | bytes 5580800
  (225 shorter events, 133.1 us)
Async XLA Ops:
  13.1 9.7 copy-start.2
  13.1 9.7 copy-start.8
  13.1 273.4 %all-to-all-start = ((bf16[32,52,3200]{2,1,0:T(8,128)(2,1)}), bf16[32,52,3200]{2,1,0:T(8,128)(2,1)}, u32[]{:S(2)}, u32[]{:S(2)}) async-start(bf16[32,52,3200]{2,1,0:T(8,128)(2,1)} %stack.3), calls=%async_computation | async-start | bytes 22937600 | tf_op jit(solution)/shard_map/all_to_all | solution.py:73
  309.0 46.5 %all-reduce.4.cloned.1.call-start = ((), (), s32[]{:S(2)}) async-start(), calls=%async_computation.1 | async-start | bytes 212992 | tf_op jit(solution)/shard_map/while/body/eval_jaxpr/psum | solution.py:122
  314.4 44.6 %collective-permute-start = (bf16[32,3200]{1,0:T(8,128)(2,1)S(1)}, bf16[32,3200]{1,0:T(8,128)(2,1)S(1)}, u32[]{:S(2)}, u32[]{:S(2)}) collective-permute-start(bf16[32,3200]{1,0:T(8,128)(2,1)S(1)} %get-tuple-element.368), channel_id=1, source_target_pairs={{64,0},{128,64},{192,128},{65,1},{129,65},{193,129},{66,2},{130,66... | collective-permute-start | bytes 614408 | tf_op jit(solution)/shard_map/while/body/eval_jaxpr/ppermute | solution.py:22
  357.6 7.1 collective-permute-start.1
  364.7 54.4 %all-reduce.4.cloned.1.call-start = ((), (), s32[]{:S(2)}) async-start(), calls=%async_computation.1 | async-start | bytes 212992 | tf_op jit(solution)/shard_map/while/body/eval_jaxpr/psum | solution.py:122
  370.0 52.5 %collective-permute-start = (bf16[32,3200]{1,0:T(8,128)(2,1)S(1)}, bf16[32,3200]{1,0:T(8,128)(2,1)S(1)}, u32[]{:S(2)}, u32[]{:S(2)}) collective-permute-start(bf16[32,3200]{1,0:T(8,128)(2,1)S(1)} %get-tuple-element.368), channel_id=1, source_target_pairs={{64,0},{128,64},{192,128},{65,1},{129,65},{193,129},{66,2},{130,66... | collective-permute-start | bytes 614408 | tf_op jit(solution)/shard_map/while/body/eval_jaxpr/ppermute | solution.py:22
  421.2 7.1 collective-permute-start.1
  428.3 56.1 %all-reduce.4.cloned.1.call-start = ((), (), s32[]{:S(2)}) async-start(), calls=%async_computation.1 | async-start | bytes 212992 | tf_op jit(solution)/shard_map/while/body/eval_jaxpr/psum | solution.py:122
  433.6 54.3 %collective-permute-start = (bf16[32,3200]{1,0:T(8,128)(2,1)S(1)}, bf16[32,3200]{1,0:T(8,128)(2,1)S(1)}, u32[]{:S(2)}, u32[]{:S(2)}) collective-permute-start(bf16[32,3200]{1,0:T(8,128)(2,1)S(1)} %get-tuple-element.368), channel_id=1, source_target_pairs={{64,0},{128,64},{192,128},{65,1},{129,65},{193,129},{66,2},{130,66... | collective-permute-start | bytes 614408 | tf_op jit(solution)/shard_map/while/body/eval_jaxpr/ppermute | solution.py:22
  486.6 7.1 collective-permute-start.1
  493.7 56.1 %all-reduce.4.cloned.1.call-start = ((), (), s32[]{:S(2)}) async-start(), calls=%async_computation.1 | async-start | bytes 212992 | tf_op jit(solution)/shard_map/while/body/eval_jaxpr/psum | solution.py:122
  507.0 63.7 %collective-permute-start = (bf16[32,3200]{1,0:T(8,128)(2,1)S(1)}, bf16[32,3200]{1,0:T(8,128)(2,1)S(1)}, u32[]{:S(2)}, u32[]{:S(2)}) collective-permute-start(bf16[32,3200]{1,0:T(8,128)(2,1)S(1)} %get-tuple-element.368), channel_id=1, source_target_pairs={{64,0},{128,64},{192,128},{65,1},{129,65},{193,129},{66,2},{130,66... | collective-permute-start | bytes 614408 | tf_op jit(solution)/shard_map/while/body/eval_jaxpr/ppermute | solution.py:22
  552.0 18.6 %collective-permute-start.1 = (bf16[32,1664]{1,0:T(8,128)(2,1)S(1)}, bf16[32,1664]{1,0:T(8,128)(2,1)S(1)}, u32[]{:S(2)}, u32[]{:S(2)}) collective-permute-start(bf16[32,1664]{1,0:T(8,128)(2,1)S(1)} %get-tuple-element.369), channel_id=1, source_target_pairs={{64,0},{128,64},{192,128},{65,1},{129,65},{193,129},{66,2},{130,66... | collective-permute-start | bytes 319496 | tf_op jit(solution)/shard_map/while/body/eval_jaxpr/ppermute | solution.py:22
  570.6 44.6 %all-reduce.4.cloned.1.call-start = ((), (), s32[]{:S(2)}) async-start(), calls=%async_computation.1 | async-start | bytes 212992 | tf_op jit(solution)/shard_map/while/body/eval_jaxpr/psum | solution.py:122
  583.9 52.1 %collective-permute-start = (bf16[32,3200]{1,0:T(8,128)(2,1)S(1)}, bf16[32,3200]{1,0:T(8,128)(2,1)S(1)}, u32[]{:S(2)}, u32[]{:S(2)}) collective-permute-start(bf16[32,3200]{1,0:T(8,128)(2,1)S(1)} %get-tuple-element.368), channel_id=1, source_target_pairs={{64,0},{128,64},{192,128},{65,1},{129,65},{193,129},{66,2},{130,66... | collective-permute-start | bytes 614408 | tf_op jit(solution)/shard_map/while/body/eval_jaxpr/ppermute | solution.py:22
  617.4 18.6 %collective-permute-start.1 = (bf16[32,1664]{1,0:T(8,128)(2,1)S(1)}, bf16[32,1664]{1,0:T(8,128)(2,1)S(1)}, u32[]{:S(2)}, u32[]{:S(2)}) collective-permute-start(bf16[32,1664]{1,0:T(8,128)(2,1)S(1)} %get-tuple-element.369), channel_id=1, source_target_pairs={{64,0},{128,64},{192,128},{65,1},{129,65},{193,129},{66,2},{130,66... | collective-permute-start | bytes 319496 | tf_op jit(solution)/shard_map/while/body/eval_jaxpr/ppermute | solution.py:22
  636.0 41.2 %all-reduce.4.cloned.1.call-start = ((), (), s32[]{:S(2)}) async-start(), calls=%async_computation.1 | async-start | bytes 212992 | tf_op jit(solution)/shard_map/while/body/eval_jaxpr/psum | solution.py:122
  649.3 48.7 %collective-permute-start = (bf16[32,3200]{1,0:T(8,128)(2,1)S(1)}, bf16[32,3200]{1,0:T(8,128)(2,1)S(1)}, u32[]{:S(2)}, u32[]{:S(2)}) collective-permute-start(bf16[32,3200]{1,0:T(8,128)(2,1)S(1)} %get-tuple-element.368), channel_id=1, source_target_pairs={{64,0},{128,64},{192,128},{65,1},{129,65},{193,129},{66,2},{130,66... | collective-permute-start | bytes 614408 | tf_op jit(solution)/shard_map/while/body/eval_jaxpr/ppermute | solution.py:22
  679.5 18.6 %collective-permute-start.1 = (bf16[32,1664]{1,0:T(8,128)(2,1)S(1)}, bf16[32,1664]{1,0:T(8,128)(2,1)S(1)}, u32[]{:S(2)}, u32[]{:S(2)}) collective-permute-start(bf16[32,1664]{1,0:T(8,128)(2,1)S(1)} %get-tuple-element.369), channel_id=1, source_target_pairs={{64,0},{128,64},{192,128},{65,1},{129,65},{193,129},{66,2},{130,66... | collective-permute-start | bytes 319496 | tf_op jit(solution)/shard_map/while/body/eval_jaxpr/ppermute | solution.py:22
  698.1 41.0 %all-reduce.4.cloned.1.call-start = ((), (), s32[]{:S(2)}) async-start(), calls=%async_computation.1 | async-start | bytes 212992 | tf_op jit(solution)/shard_map/while/body/eval_jaxpr/psum | solution.py:122
  711.4 48.5 %collective-permute-start = (bf16[32,3200]{1,0:T(8,128)(2,1)S(1)}, bf16[32,3200]{1,0:T(8,128)(2,1)S(1)}, u32[]{:S(2)}, u32[]{:S(2)}) collective-permute-start(bf16[32,3200]{1,0:T(8,128)(2,1)S(1)} %get-tuple-element.368), channel_id=1, source_target_pairs={{64,0},{128,64},{192,128},{65,1},{129,65},{193,129},{66,2},{130,66... | collective-permute-start | bytes 614408 | tf_op jit(solution)/shard_map/while/body/eval_jaxpr/ppermute | solution.py:22
  741.2 18.6 %collective-permute-start.1 = (bf16[32,1664]{1,0:T(8,128)(2,1)S(1)}, bf16[32,1664]{1,0:T(8,128)(2,1)S(1)}, u32[]{:S(2)}, u32[]{:S(2)}) collective-permute-start(bf16[32,1664]{1,0:T(8,128)(2,1)S(1)} %get-tuple-element.369), channel_id=1, source_target_pairs={{64,0},{128,64},{192,128},{65,1},{129,65},{193,129},{66,2},{130,66... | collective-permute-start | bytes 319496 | tf_op jit(solution)/shard_map/while/body/eval_jaxpr/ppermute | solution.py:22
  772.1 152.5 %copy-start.9 = (u32[256]{0:T(256)S(1)}, u32[256]{0:T(256)}, u32[]{:S(2)}) copy-start(u32[256]{0:T(256)} %constant.123) | copy-start | bytes 3076
  922.7 26.2 %collective-permute-start.7 = (bf16[52,3200]{1,0:T(8,128)(2,1)S(1)}, bf16[52,3200]{1,0:T(8,128)(2,1)S(1)}, u32[]{:S(2)}, u32[]{:S(2)}) collective-permute-start(bf16[52,3200]{1,0:T(8,128)(2,1)S(1)} %slice.4), channel_id=1, source_target_pairs={{0,12},{2,14},{4,16},{6,18},{8,20},{10,22},{12,24},{14,26},{16,28}... | collective-permute-start | bytes 998408
  925.9 33.6 %collective-permute-start.2 = (bf16[64,3200]{1,0:T(8,128)(2,1)S(1)}, bf16[64,3200]{1,0:T(8,128)(2,1)S(1)}, u32[]{:S(2)}, u32[]{:S(2)}) collective-permute-start(bf16[64,3200]{1,0:T(8,128)(2,1)S(1)} %fusion), channel_id=1, source_target_pairs={{0,2},{2,4},{4,6},{6,8},{8,10},{10,12},{12,14},{14,16},{16,18},{18... | collective-permute-start | bytes 1228808
  927.8 33.1 %collective-permute-start.3 = (bf16[64,3200]{1,0:T(8,128)(2,1)S(1)}, bf16[64,3200]{1,0:T(8,128)(2,1)S(1)}, u32[]{:S(2)}, u32[]{:S(2)}) collective-permute-start(bf16[64,3200]{1,0:T(8,128)(2,1)S(1)} %fusion), channel_id=1, source_target_pairs={{0,4},{2,6},{4,8},{6,10},{8,12},{10,14},{12,16},{14,18},{16,20},{1... | collective-permute-start | bytes 1228808
  933.5 27.3 %collective-permute-start.4 = (bf16[64,3200]{1,0:T(8,128)(2,1)S(1)}, bf16[64,3200]{1,0:T(8,128)(2,1)S(1)}, u32[]{:S(2)}, u32[]{:S(2)}) collective-permute-start(bf16[64,3200]{1,0:T(8,128)(2,1)S(1)} %fusion), channel_id=1, source_target_pairs={{0,6},{2,8},{4,10},{6,12},{8,14},{10,16},{12,18},{14,20},{16,22},{... | collective-permute-start | bytes 1228808
  935.5 25.4 %collective-permute-start.5 = (bf16[64,3200]{1,0:T(8,128)(2,1)S(1)}, bf16[64,3200]{1,0:T(8,128)(2,1)S(1)}, u32[]{:S(2)}, u32[]{:S(2)}) collective-permute-start(bf16[64,3200]{1,0:T(8,128)(2,1)S(1)} %fusion), channel_id=1, source_target_pairs={{0,8},{2,10},{4,12},{6,14},{8,16},{10,18},{12,20},{14,22},{16,24},... | collective-permute-start | bytes 1228808
  948.9 12.0 %copy-start.7 = (bf16[52,3200]{1,0:T(8,128)(2,1)}, bf16[52,3200]{1,0:T(8,128)(2,1)S(1)}, u32[]{:S(2)}) copy-start(bf16[52,3200]{1,0:T(8,128)(2,1)S(1)} %collective-permute-done.7) | copy-start | bytes 998404
  948.9 59.8 %collective-permute-start.6 = (bf16[64,3200]{1,0:T(8,128)(2,1)S(1)}, bf16[64,3200]{1,0:T(8,128)(2,1)}, u32[]{:S(2)}, u32[]{:S(2)}) collective-permute-start(bf16[64,3200]{1,0:T(8,128)(2,1)S(1)} %fusion), channel_id=1, source_target_pairs={{0,10},{2,12},{4,14},{6,16},{8,18},{10,20},{12,22},{14,24},{16,26}... | collective-permute-start | bytes 1228808
  (13 other events, 26.5 us)
Sparse Core Ops, SparseCore 0:
  314.5 40.8 all-reduce.3
  370.1 48.8 all-reduce.3
  433.8 50.6 all-reduce.3
  507.1 42.6 all-reduce.3
  584.1 31.1 all-reduce.3
  649.5 27.7 all-reduce.3
  711.5 27.4 all-reduce.3
